TPU v7x, 256 devices: a whole 4x4x8 slice. The times are simulated.
256 devices in a mesh: blk: 64 (over y, z, x_lo), rep: 4 (over x_hi, core).
Axes of the slice: x: 4 (x_hi: 2, x_lo: 2; x = x_hi * 2 + x_lo), y: 4, z: 8, core: 2. Of those that a mesh axis runs over, the one named last changes fastest.
Arguments:
- layer_input: bfloat16 [98304, 8192], P(('blk', 'rep')), may hold values from -24 to 24
- norm_gain: bfloat16 [8192], replicated, may hold values from 0.099609375 to 1.8984375
- key_cotangent: bfloat16 [98304, 512], P(('blk', 'rep')), may hold values from -6 to 6
- segment_ids: int32 [98304], P(('blk', 'rep')), may hold values from 0 to 2
- key_weight: bfloat16 [8192, 512], P('blk'), may hold values from -0.0625 to 0.0625
Outputs:
- weight_grad: float32 [8192, 512], P('blk')
- input_grad: bfloat16 [98304, 8192], P(('blk', 'rep'))
All inputs are finite; a program needn't handle non-finite values.
Results may differ from a plain program's by a relative error of at most 0.0029.
Values may be sent and summed in bfloat16 or wider, within the bound.
A program may use at most 128 MiB of HBM per device.

v0:
```python
import jax
import jax.numpy as jnp
from jax import lax
from jax.sharding import PartitionSpec as P


def on_device(layer_input, norm_gain, key_cotangent, segment_ids, key_weight):
    tokens_here, width = layer_input.shape
    xs = layer_input.astype(jnp.float32)
    gain = norm_gain.astype(jnp.float32)
    rstd = lax.rsqrt(jnp.mean(xs * xs, axis=1, keepdims=True) + 1e-05)
    normed = (xs * rstd * gain).astype(jnp.bfloat16)
    live = jnp.where((segment_ids != 0)[:, None], key_cotangent, jnp.zeros_like(key_cotangent))
    normed_grad = lax.dot_general(
        live,
        lax.all_gather(key_weight, "blk", axis=0, tiled=True),
        (((1,), (1,)), ((), ())),
        preferred_element_type=jnp.float32,
    )
    inner = jnp.sum(xs * gain * normed_grad, axis=1, keepdims=True)
    input_grad = (rstd * gain * normed_grad - xs * rstd**3 * inner / width).astype(jnp.bfloat16)
    total_tokens = tokens_here * lax.axis_size("blk") * lax.axis_size("rep")
    share = lax.psum_scatter(
        lax.dot_general(normed, live, (((0,), (0,)), ((), ())), preferred_element_type=jnp.float32),
        "blk",
        scatter_dimension=0,
        tiled=True,
    )
    summed = lax.psum(share, "rep")
    weight_grad = summed / jnp.sqrt(jnp.float32(total_tokens))
    return (weight_grad, input_grad)


def solution(mesh):
    placed = (
        P(("blk", "rep"), None),
        P(),
        P(("blk", "rep"), None),
        P(("blk", "rep")),
        P("blk", None),
    )
    return jax.shard_map(
        on_device,
        mesh=mesh,
        in_specs=placed,
        out_specs=(P("blk", None), P(("blk", "rep"), None)),
        check_vma=False,
    )
```

profile of v0, /device:TPU:1, one launch (start us, length us, event | category | flops | bytes accessed | tf_op | source)
XLA Modules:
  0.0 769.2 jit_solution(17473573303249687480)
XLA Ops:
  7.2 0.0 all-gather.2.cloned.1.call-start
  7.2 0.7 all-gather.2.cloned.1.call-update
  7.9 0.0 reduce-scatter.2.cloned.1.call-start
  7.9 0.7 convert_element_type.13
  8.7 0.7 broadcast_compare_fusion
  9.4 0.0 copy-start.1
  9.4 278.1 %all-gather.2.cloned.1.call-done = bf16[8192,512]{1,0:T(8,128)(2,1)} async-done(((bf16[128,512]{1,0:T(8,128)(2,1)}), bf16[8192,512]{1,0:T(8,128)(2,1)}) %all-gather.2.cloned.1.call-update) | async-done | bytes 8388624 | tf_op jit(solution)/shard_map/all_gather | solution.py:16
  287.5 0.0 copy-start
  287.5 10.3 %fusion.8 = (f32[384]{0:T(512)S(1)}, f32[384]{0:T(512)S(1)}, f32[384,8192]{1,0:T(8,128)}) fusion(bf16[384,8192]{1,0:T(8,128)(2,1)} %param.5, f32[8192]{0:T(1024)S(1)} %convert_element_type.13, bf16[8192,512]{1,0:T(8,128)(2,1)} %all-gather.2.cloned.1.call-done, bf16[384,512]{1,0:T(8,128)(2,1)} %param.7, pred[384]{0:T(512)(128)(4,1)S(1)} %broadcast_compare_fusion), kind=kOutput, calls=%fused_computation.12 | convolution fusion | flops 3240295424 | bytes 27692416 | tf_op jit(solution)/shard_map/dot_general | solution.py:14
  297.8 0.0 copy-done.1
  297.8 0.0 copy-done
  297.8 8.3 %fusion.9 = f32[8192,512]{1,0:T(8,128)} fusion(bf16[384,8192]{1,0:T(8,128)(2,1)S(1)} %copy-done, f32[8192]{0:T(1024)S(1)} %convert_element_type.13, f32[384]{0:T(512)S(1)} %get-tuple-element.5, bf16[384,512]{1,0:T(8,128)(2,1)S(1)} %copy-done.1, pred[384]{0:T(512)(128)(4,1)S(1)} %broadcast_compare_fusion), kind=kOutput, calls=%fused_computation.13 | convolution fusion | flops 3234004992 | bytes 23496576 | tf_op jit(solution)/shard_map/dot_general | solution.py:24
  306.1 0.0 reduce-scatter.2.cloned.1.call-update
  306.2 0.0 all-reduce.2.cloned.1.call-start
  306.2 405.1 %reduce-scatter.2.cloned.1.call-done = f32[128,512]{1,0:T(8,128)} async-done(((f32[8192,512]{1,0:T(8,128)}), f32[128,512]{1,0:T(8,128)}) %reduce-scatter.2.cloned.1.call-update) | async-done | bytes 262160 | tf_op jit(solution)/shard_map/reduce_scatter | solution.py:23
  711.3 0.0 all-reduce.2.cloned.1.call-update
  711.3 11.2 %fusion.6 = bf16[384,8192]{1,0:T(8,128)(2,1)} fusion(bf16[384,8192]{1,0:T(8,128)(2,1)} %param.5, f32[384,8192]{1,0:T(8,128)} %get-tuple-element.6, f32[384]{0:T(512)S(1)} %get-tuple-element.2, f32[384]{0:T(512)S(1)} %get-tuple-element.4, f32[8192]{0:T(1024)S(1)} %convert_element_type.13, f32[384]{0:T(512)S(1)} %get-tuple-element.5), kind=kLoop, calls=%fused_computation.10 | loop fusion | flops 25165824 | bytes 25203200 | tf_op jit(solution)/shard_map/convert_element_type | solution.py:21
  722.5 38.5 %all-reduce.2.cloned.1.call-done = f32[128,512]{1,0:T(8,128)} async-done(((f32[128,512]{1,0:T(8,128)}), f32[128,512]{1,0:T(8,128)}) %all-reduce.2.cloned.1.call-update) | async-done | bytes 262160 | tf_op jit(solution)/shard_map/psum | solution.py:29
  761.0 1.7 broadcast_multiply_fusion
  (1 shorter events, 0.0 us)
Async XLA Ops:
  7.2 280.3 %all-gather.2.cloned.1.call-start = ((), (), s32[]{:S(2)}) async-start(), calls=%async_computation.3 | async-start | bytes 8519680 | tf_op jit(solution)/shard_map/all_gather | solution.py:16
  7.9 703.4 %reduce-scatter.2.cloned.1.call-start = ((), (), s32[]{:S(2)}) async-start(), calls=%async_computation.1 | async-start | bytes 17039360 | tf_op jit(solution)/shard_map/reduce_scatter | solution.py:23
  9.4 288.5 %copy-start.1 = (bf16[384,512]{1,0:T(8,128)(2,1)S(1)}, bf16[384,512]{1,0:T(8,128)(2,1)}, u32[]{:S(2)}) copy-start(bf16[384,512]{1,0:T(8,128)(2,1)} %param.7) | copy-start | bytes 1179652
  287.5 10.4 %copy-start = (bf16[384,8192]{1,0:T(8,128)(2,1)S(1)}, bf16[384,8192]{1,0:T(8,128)(2,1)}, u32[]{:S(2)}) copy-start(bf16[384,8192]{1,0:T(8,128)(2,1)} %param.5) | copy-start | bytes 18874372
  306.2 454.9 %all-reduce.2.cloned.1.call-start = ((), (), s32[]{:S(2)}) async-start(), calls=%async_computation.2 | async-start | bytes 524288 | tf_op jit(solution)/shard_map/psum | solution.py:29
Sparse Core Ops, SparseCore 0:
  9.8 277.6 all-gather.1
  306.3 404.9 reduce-scatter.1
  713.9 47.0 all-reduce.1
where the time goes:
time: 769 us
  waiting for transfers between devices  722 us (94%)
  matrix products  18.6 us (2%)
  other arithmetic  14.3 us (2%)
  between operations  13.8 us (2%)
    reduce_scatter x1, waiting for transfers between devices, on_device(): lax.psum_scatter(lax.dot_general(normed, live, (((0,), (0,)), ((), ())),...  405 us
    all_gather x1, waiting for transfers between devices, on_device(): lax.all_gather(key_weight, 'blk', axis=0, tiled=True)  278 us
    psum x1, waiting for transfers between devices, on_device(): summed = lax.psum(share, 'rep')  38.5 us
  transfers between devices with their start and end apart: 3, of which 3 were waited for; matrix products, arithmetic and copies ran while one was open for 2% of the time, Pallas kernels for 0%

commit v1 on v0

v1 whole, which is shorter than its diff:
```python
import jax
import jax.numpy as jnp
from jax import lax
from jax.experimental import pallas as pl
from jax.experimental.pallas import tpu as pltpu
from jax.sharding import PartitionSpec as P

F32 = jnp.float32
BF16 = jnp.bfloat16
NX, NY, NZ = 4, 4, 8
TOK, D, KW, TOKENS = 384, 8192, 512, 98304
CH = 256
NCH = D // CH


def dev(x, y, z, c):
    return {"blk": (y * NZ + z) * 2 + x % 2, "rep": (x // 2) * 2 + c}


class Ring:
    def __init__(self, own, subs, plus, minus, send, recv, ssem, rsem):
        self.own, self.subs, self.to = own, subs, (plus, minus)
        self.send, self.recv, self.ssem, self.rsem = send, recv, ssem, rsem

    def copy(self, i):
        return pltpu.make_async_remote_copy(
            self.send.at[i], self.recv.at[i], self.ssem.at[i], self.rsem.at[i], device_id=self.to[i % 2]
        )

    def put(self, i, rel, h, plus=None):
        for s in range(self.subs):
            v = self.own(rel, h, s)
            if plus is not None:
                v = v + self.recv[plus, s].astype(F32)
            self.send[i, s] = v.astype(self.send.dtype)
        self.copy(i).start()

    def far(self, h):
        self.put(h, 2, h)

    def single(self, d):
        self.put(2 + d, (1, 3)[d], (1, 0)[d])

    def combine(self, d):
        self.copy(d).wait_recv()
        self.put(4 + d, (1, 3)[d], d, plus=d)

    def mine_wait(self, h):
        for i in ((4, 3), (2, 5))[h]:
            self.copy(i).wait_recv()

    def mine(self, h, s):
        a, b = ((4, 3), (2, 5))[h]
        return self.own(0, h, s) + self.recv[a, s].astype(F32) + self.recv[b, s].astype(F32)

    def finish(self):
        for i in range(6):
            self.copy(i).wait_send()


def kernel(
    x_hbm, gain_ref, live_ref, w_hbm, wg_ref, ig_hbm,
    X, Wf, Nh, Ns, LT, S, NG, ACC, RB, A2, B2, T, Tb, ZR, O,
    r1x_s, r1x_r, r1y_s, r1y_r, r2y_s, r2y_r, r2x_s, r2x_r,
    xsem, wsem, osem, nss, nsr, lts, ltr,
    axs, axr, ays, ayr, zs, zr, shs, shr, sys_, syr,
    q1xs, q1xr, q1ys, q1yr, q2ys, q2yr, q2xs, q2xr,
    zds, zdr, fs, fr,
):
    b, r = lax.axis_index("blk"), lax.axis_index("rep")
    xl, z, y = b % 2, (b // 2) % NZ, b // (2 * NZ)
    xh, c = r // 2, r % 2
    x = 2 * xh + xl
    sib = dev(x, y, z, 1 - c)
    xp, xm = dev((x + 1) % 4, y, z, c), dev((x + 3) % 4, y, z, c)
    yp, ym = dev(x, (y + 1) % 4, z, c), dev(x, (y + 3) % 4, z, c)
    zp, zm = dev(x, y, (z + 1) % 8, c), dev(x, y, (z + 7) % 8, c)
    far_same, far_other = dev((x + 2) % 4, y, z, c), dev((x + 2) % 4, y, z, 1 - c)

    wcp = pltpu.make_async_copy(w_hbm, Wf.at[y, z, xl], wsem)
    wcp.start()

    def xcopy(j):
        return pltpu.make_async_copy(x_hbm.at[:, pl.ds(pl.multiple_of(j * CH, CH), CH)], X.at[j], xsem.at[j])

    lax.fori_loop(0, NCH, lambda j, u: (xcopy(j).start(), u)[1], 0)

    bar = pltpu.get_barrier_semaphore()
    met = [sib, xp, xm, yp, ym, far_same, far_other] + [dev(x, y, (z + k) % 8, c) for k in range(1, 8)]
    for d in met:
        pl.semaphore_signal(bar, 1, device_id=d)
    pl.semaphore_wait(bar, len(met))

    full, h0, h1 = pl.ds(64 * c, 64), pl.ds(64 * c, 32), pl.ds(64 * c + 32, 32)
    sfull, sh0, sh1 = pl.ds(64 - 64 * c, 64), pl.ds(64 - 64 * c, 32), pl.ds(96 - 64 * c, 32)
    col_y = (y, y, (y + 3) % 4, (y + 1) % 4, (y + 2) % 4)

    def region(col, zz, rows):
        if col == 0:
            return Wf.at[y, zz, xl, rows]
        if col == 1:
            return Wf.at[y, zz, 1 - xl, rows]
        return Wf.at[col_y[col], zz, :, rows]

    def rcopy(src, dst, ss, rs, to):
        return pltpu.make_async_remote_copy(src, dst, ss, rs, device_id=to)

    def same(ref, ss, rs, to):
        return rcopy(ref, ref, ss, rs, to)

    ax_out = [same(Wf.at[y, z, xl, h0], axs.at[0], axr.at[0], xp), same(Wf.at[y, z, xl, h1], axs.at[1], axr.at[1], xm)]
    ax_in = [
        rcopy(Wf.at[y, z, 1 - xl, h0], Wf.at[y, z, 1 - xl, h0], axs.at[0], axr.at[0], xp),
        rcopy(Wf.at[y, z, 1 - xl, h1], Wf.at[y, z, 1 - xl, h1], axs.at[1], axr.at[1], xm),
    ]
    own_pair = Wf.at[y, z, :, full]
    ay_out = [
        same(own_pair, ays.at[0], ayr.at[0], yp),
        same(own_pair, ays.at[1], ayr.at[1], ym),
        same(Wf.at[(y + 3) % 4, z, :, h0], ays.at[2], ayr.at[2], yp),
        same(Wf.at[(y + 1) % 4, z, :, h1], ays.at[3], ayr.at[3], ym),
    ]
    ay_in = [
        same(Wf.at[(y + 3) % 4, z, :, full], ays.at[0], ayr.at[0], yp),
        same(Wf.at[(y + 1) % 4, z, :, full], ays.at[1], ayr.at[1], ym),
        same(Wf.at[(y + 2) % 4, z, :, h0], ays.at[2], ayr.at[2], yp),
        same(Wf.at[(y + 2) % 4, z, :, h1], ays.at[3], ayr.at[3], ym),
    ]

    def z_at(d, k):
        return (z + 8 - k) % 8 if d == 0 else (z + k) % 8

    def z_out(col, d, k):
        rows = full if k < 4 else (h0, h1)[d]
        return same(region(col, z_at(d, k - 1), rows), zs.at[col, d, k - 1], zr.at[col, d, k - 1], (zp, zm)[d])

    def z_in(col, d, k):
        rows = full if k < 4 else (h0, h1)[d]
        return same(region(col, z_at(d, k), rows), zs.at[col, d, k - 1], zr.at[col, d, k - 1], (zp, zm)[d])

    def share(col, d, k):
        rows = full if k < 4 else (h0, h1)[d]
        return same(region(col, z_at(d, k), rows), shs.at[col, d, k - 1], shr.at[col, d, k - 1], sib)

    def share_in(col, d, k):
        rows = sfull if k < 4 else (sh0, sh1)[d]
        return same(region(col, z_at(d, k), rows), shs.at[col, d, k - 1], shr.at[col, d, k - 1], sib)

    def share_own(col):
        return same(region(col, z, full), sys_.at[col - 1], syr.at[col - 1], sib)

    def share_own_in(col):
        return same(region(col, z, sfull), sys_.at[col - 1], syr.at[col - 1], sib)

    def z_first(col):
        z_out(col, 0, 1).start()
        z_out(col, 1, 1).start()

    def z_serve(k, cols):
        for col in cols:
            for d in range(2):
                z_in(col, d, k).wait_recv()
                if k < 4:
                    z_out(col, d, k + 1).start()
                share(col, d, k).start()

    wcp.wait()
    for cp in ax_out:
        cp.start()
    z_first(0)

    ACC[...] = jnp.zeros_like(ACC)

    def ssq(g, u):
        tot = jnp.zeros((TOK, 128), F32)
        for i in range(4):
            xcopy(g * 4 + i).wait()
            v = X[g * 4 + i].astype(F32)
            v = v * v
            tot = tot + (v[:, :128] + v[:, 128:])
        ACC[...] += tot
        return u

    lax.fori_loop(0, NCH // 4, ssq, 0)
    mean = jnp.sum(ACC[...], axis=1, keepdims=True) / D
    rstd = lax.rsqrt(mean + 1e-05)
    RB[...] = jnp.broadcast_to(rstd, (TOK, 128))

    for cp in ax_in:
        cp.wait_recv()
    for cp in ay_out[:2]:
        cp.start()
    z_first(1)
    share_own(1).start()

    LT[:, 0:TOK] = live_ref[...].astype(F32).T.astype(BF16)
    lt_copy = rcopy(LT.at[:, 0:TOK], LT.at[:, TOK : 2 * TOK], lts, ltr, sib)
    lt_copy.start()

    def normed(j):
        rb = RB[...]
        v = X[j].astype(F32)
        return (v * jnp.concatenate([rb, rb], axis=1) * gain_ref[j]).astype(BF16)

    def n_copy(i):
        return rcopy(Ns.at[i], Nh.at[i, TOK : 2 * TOK], nss.at[i], nsr.at[i], sib)

    def order(i):
        far = i < 2
        mid = i < 10
        yy = jnp.where(far, (y + 2) % 4, jnp.where(mid, (i - 2) % 4, (y + jnp.where(i < 12, 1, jnp.where(i < 14, 3, 0))) % 4))
        zz = jnp.where(far, 2 + i, jnp.where(mid, (i - 2) // 4, 2 + i % 2))
        return yy, zz

    def norm_sib(i, u):
        yy, zz = order(i)
        Ns[yy * 4 + zz] = normed(yy * 8 + 4 * (1 - c) + zz)
        n_copy(yy * 4 + zz).start()
        return u

    def norm_own(i, u):
        yy, zz = order(i)
        Nh[yy * 4 + zz, 0:TOK] = normed(yy * 8 + 4 * c + zz)
        return u

    lax.fori_loop(0, 16, norm_sib, 0)
    for i in range(2):
        ay_in[i].wait_recv()
        ay_out[2 + i].start()
    for col in (2, 3):
        z_first(col)
        share_own(col).start()
    lax.fori_loop(0, 16, norm_own, 0)
    for cp in ay_in[2:]:
        cp.wait_recv()
    z_first(4)
    share_own(4).start()
    lt_copy.wait_recv()

    def product(i, u):
        yy, zz = order(i)
        at = yy * 4 + zz
        n_copy(at).wait_recv()
        st = jnp.dot(LT[...], Nh[at], preferred_element_type=F32)
        S[at, 0] = st[:, :128]
        S[at, 1] = st[:, 128:]
        return u

    def x_of(rel):
        xx = (x + rel) % 4
        return xx % 2, xx // 2

    def own_1x(rel, h, s):
        l, hi = x_of(rel)
        return S[s * 4 + h, l, pl.ds(pl.multiple_of(256 * hi, 256), 256)]

    def own_1y(rel, h, s):
        return S[((y + rel) % 4) * 4 + 2 + h, s // 2, 256 * (s % 2) : 256 * (s % 2) + 256]

    def own_2y(rel, h, s):
        return A2[h, (y + rel) % 4]

    def own_2x(rel, h, s):
        l, hi = x_of(rel)
        return B2[h, l * 2 + hi]

    r1x = Ring(own_1x, 4, xp, xm, r1x_s, r1x_r, q1xs, q1xr)
    r1y = Ring(own_1y, 4, yp, ym, r1y_s, r1y_r, q1ys, q1yr)
    r2y = Ring(own_2y, 1, yp, ym, r2y_s, r2y_r, q2ys, q2yr)
    r2x = Ring(own_2x, 1, xp, xm, r2x_s, r2x_r, q2xs, q2xr)

    lax.fori_loop(0, 2, product, 0)
    r1y.far(0)
    r1y.far(1)
    lax.fori_loop(2, 6, product, 0)
    r1x.far(0)
    r1x.single(1)
    lax.fori_loop(6, 10, product, 0)
    r1x.far(1)
    r1x.single(0)
    z_serve(1, (0, 1))
    lax.fori_loop(10, 14, product, 0)
    r1y.single(0)
    r1y.single(1)
    lax.fori_loop(14, 16, product, 0)
    z_serve(1, (2, 3))
    r1y.combine(0)
    r1y.combine(1)
    r1x.combine(0)
    r1x.combine(1)
    z_serve(1, (4,))

    ACC[...] = jnp.zeros_like(ACC)

    def ng_chunk(yy, zz):
        j = yy * 8 + zz
        w = Wf[yy, zz].reshape(CH, KW)
        ng = lax.dot_general(live_ref[...], w, (((1,), (1,)), ((), ())), preferred_element_type=F32)
        NG[j] = ng
        v = X[j].astype(F32) * gain_ref[j] * ng
        ACC[...] += v[:, :128] + v[:, 128:]

    for col in (1, 2, 3, 4):
        share_own_in(col).wait_recv()
    lax.fori_loop(0, 4, lambda yy, u: (ng_chunk(yy, z), u)[1], 0)

    def ng_step(k):
        for col in range(5):
            for d in range(2):
                share_in(col, d, k).wait_recv()
        for d in range(2 if k < 4 else 1):
            lax.fori_loop(0, 4, lambda yy, u, d=d: (ng_chunk(yy, z_at(d, k)), u)[1], 0)

    ng_step(1)

    for h in range(2):
        r1y.mine_wait(h)
        for s in range(4):
            B2[h, s] = r1y.mine(h, s)
        r2x.far(h)
        r2x.single(1 - h)
    for h in range(2):
        r1x.mine_wait(h)
        for s in range(4):
            A2[h, s] = r1x.mine(h, s)
        r2y.far(h)
        r2y.single(1 - h)

    z_serve(2, range(5))
    r2x.combine(0)
    r2x.combine(1)
    r2y.combine(0)
    r2y.combine(1)
    ng_step(2)

    for h in range(2):
        r2y.mine_wait(h)
        T[h] = r2y.mine(h, 0)
        r2x.mine_wait(h)
        T[2 + h] = r2x.mine(h, 0)

    def zd_copy(k):
        return rcopy(Tb.at[k], ZR.at[z], zds.at[k], zdr.at[z], dev(x, y, 4 * c + k, c))

    for k in range(4):
        @pl.when(4 * c + k != z)
        def _(k=k):
            Tb[k] = T[k].astype(BF16)
            zd_copy(k).start()

    z_serve(3, range(5))
    ng_step(3)

    owner = z // 4 == c

    def out_copy(i):
        to = (sib, far_same, far_other)[i]
        return rcopy(O.at[xh], O.at[xh], fs.at[i], fr.at[jnp.where(i == 0, 0, 1)], to)

    @pl.when(owner)
    def _():
        tot = T[z % 4]
        for s in range(8):
            @pl.when(s != z)
            def _(s=s):
                rcopy(Tb.at[0], ZR.at[s], zds.at[0], zdr.at[s], sib).wait_recv()
        ZR[z] = jnp.zeros((256, 128), BF16)
        for s in range(8):
            tot = tot + ZR[s].astype(F32)
        O[xh] = (tot / jnp.sqrt(F32(TOKENS))).T
        for i in range(3):
            out_copy(i).start()

    z_serve(4, range(5))
    ng_step(4)

    inner = jnp.sum(ACC[...], axis=1, keepdims=True)
    rb = RB[...]
    ACC[...] = rb * rb * rb * jnp.broadcast_to(inner, (TOK, 128)) / D

    def o_copy(j):
        return pltpu.make_async_copy(X.at[j], ig_hbm.at[:, pl.ds(pl.multiple_of(j * CH, CH), CH)], osem.at[j])

    def last(j, u):
        rb, co = RB[...], ACC[...]
        v = X[j].astype(F32)
        g = gain_ref[j]
        out = jnp.concatenate([rb, rb], axis=1) * g * NG[j] - v * jnp.concatenate([co, co], axis=1)
        X[j] = out.astype(BF16)
        o_copy(j).start()
        return u

    lax.fori_loop(0, NCH, last, 0)

    @pl.when(jnp.logical_not(owner))
    def _():
        rcopy(O.at[xh], O.at[xh], fs.at[0], fr.at[0], sib).wait_recv()

    rcopy(O.at[1 - xh], O.at[1 - xh], fs.at[1], fr.at[1], far_same).wait_recv()
    wg_ref[:, 0:256] = O[0]
    wg_ref[:, 256:512] = O[1]

    @pl.when(owner)
    def _():
        for i in range(3):
            out_copy(i).wait_send()

    for k in range(4):
        @pl.when(4 * c + k != z)
        def _(k=k):
            zd_copy(k).wait_send()
    for ring in (r1x, r1y, r2x, r2y):
        ring.finish()
    for cp in ax_out + ay_out:
        cp.wait_send()
    for col in range(5):
        for d in range(2):
            for k in range(1, 5):
                z_out(col, d, k).wait_send()
                share(col, d, k).wait_send()
    for col in range(1, 5):
        share_own(col).wait_send()
    lt_copy.wait_send()
    lax.fori_loop(0, 16, lambda i, u: (n_copy(i).wait_send(), u)[1], 0)
    lax.fori_loop(0, NCH, lambda j, u: (o_copy(j).wait(), u)[1], 0)


def on_device(layer_input, norm_gain, key_cotangent, segment_ids, key_weight):
    live = jnp.where((segment_ids != 0)[:, None], key_cotangent, jnp.zeros_like(key_cotangent))
    gain = norm_gain.astype(F32).reshape(NCH, 1, CH)
    dma = pltpu.SemaphoreType.DMA
    vm = pltpu.VMEM

    def ring(subs, dtype):
        return [vm((6, subs, 256, 128), dtype)] * 2

    scratch = [
        vm((NCH, TOK, CH), BF16),
        vm((NY, NZ, 2, 128, KW), BF16),
        vm((16, 2 * TOK, CH), BF16),
        vm((16, TOK, CH), BF16),
        vm((KW, 2 * TOK), BF16),
        vm((16, 2, KW, 128), F32),
        vm((NCH, TOK, CH), F32),
        vm((TOK, 128), F32),
        vm((TOK, 128), F32),
        vm((2, 4, 256, 128), F32),
        vm((2, 4, 256, 128), F32),
        vm((4, 256, 128), F32),
        vm((4, 256, 128), BF16),
        vm((8, 256, 128), BF16),
        vm((2, 128, 256), F32),
        *ring(4, BF16), *ring(4, BF16), *ring(1, F32), *ring(1, F32),
        dma((NCH,)), dma, dma((NCH,)), dma((16,)), dma((16,)), dma, dma,
        dma((2,)), dma((2,)), dma((4,)), dma((4,)),
        dma((5, 2, 4)), dma((5, 2, 4)), dma((5, 2, 4)), dma((5, 2, 4)), dma((4,)), dma((4,)),
        *[dma((6,))] * 8,
        dma((4,)), dma((8,)), dma((3,)), dma((2,)),
    ]
    anyspace = pl.BlockSpec(memory_space=pl.ANY)
    vspace = pl.BlockSpec(memory_space=pltpu.VMEM)
    return pl.pallas_call(
        kernel,
        name="key_projection_backward",
        out_shape=(jax.ShapeDtypeStruct((128, KW), F32), jax.ShapeDtypeStruct((TOK, D), BF16)),
        in_specs=[anyspace, vspace, vspace, anyspace],
        out_specs=(vspace, anyspace),
        scratch_shapes=scratch,
        compiler_params=pltpu.CompilerParams(
            collective_id=0, has_side_effects=True, vmem_limit_bytes=62 * 2**20
        ),
    )(layer_input, gain, live, key_weight)


def solution(mesh):
    placed = (
        P(("blk", "rep"), None),
        P(),
        P(("blk", "rep"), None),
        P(("blk", "rep")),
        P("blk", None),
    )
    return jax.shard_map(
        on_device,
        mesh=mesh,
        in_specs=placed,
        out_specs=(P("blk", None), P(("blk", "rep"), None)),
        check_vma=False,
    )
```

time: 769 us -> 89.9 us (0.12)
  waiting for transfers between devices: 722 us -> 0 us
  Pallas kernels: 0 us -> 77.3 us
  matrix products: 18.6 us -> 0 us
  between operations: 13.8 us -> 0.64 us
  other arithmetic: 14.3 us -> 3.88 us
  local copies, waits for them, and re-layouts: 0.01 us -> 7.87 us
    reduce_scatter x1 -> x0, waiting for transfers between devices: 405 us -> none  [on_device(): lax.psum_scatter(lax.dot_general(normed, live, (((0,), (0,)), ((), ())),...]
    all_gather x1 -> x0, waiting for transfers between devices: 278 us -> none  [on_device(): lax.all_gather(key_weight, 'blk', axis=0, tiled=True)]
    pallas_call x0 -> x1, Pallas kernels: none -> 77.3 us  [on_device(): pl.pallas_call(kernel, name='key_projection_backward', out_shape=(jax.Sha...]
    psum x1 -> x0, waiting for transfers between devices: 38.5 us -> none  [on_device(): summed = lax.psum(share, 'rep')]
    dot_general x2 -> x0, matrix products: 18.6 us -> none  [the longest x1 10.3 us: on_device(): lax.dot_general(live, lax.all_gather(key_weight, 'blk', axis=0, tiled=Tru...]
    convert_element_type x2 -> x0, other arithmetic: 11.9 us -> none  [the longest x1 11.2 us: on_device(): (rstd * gain * normed_grad - xs * rstd ** 3 * inner / width).astype(jnp.b...]
    unnamed x4 -> x2, local copies, waits for them, and re-layouts: 0.01 us -> 7.87 us
  transfers between devices with their start and end apart: 3 -> 0, of which waited for: 3 -> 0; matrix products, arithmetic and copies ran while one was open for 2% -> 0% of each run, Pallas kernels for 0% -> 0%
where the time goes in v1:
time: 89.9 us; the launch traced here: 89.6 us
  Pallas kernels  77.3 us (86%)
  local copies, waits for them, and re-layouts  7.87 us (9%)
  other arithmetic  3.88 us (4%)
    pallas_call x1, Pallas kernels, on_device(): pl.pallas_call(kernel, name='key_projection_backward', out_shape=(jax.Sha...  77.3 us
    unnamed x2, local copies, waits for them, and re-layouts  7.87 us
    select_n x1, other arithmetic, on_device(): jnp.where((segment_ids != 0)[:, None], key_cotangent, jnp.zeros_like(key_...  1.86 us

profile of v1, /device:TPU:1, one launch (start us, length us, event | category | flops | bytes accessed | tf_op | source)
XLA Modules:
  0.0 89.6 jit_solution(12253874622217913842)
XLA Ops:
  0.6 0.7 broadcast_compare_fusion
  1.3 1.3 %reshape.12 = f32[8192]{0:T(1024)} convert(bf16[8192]{0:T(1024)(128)(2,1)} %param.6) | non-fusion elementwise | flops 8192 | bytes 49152 | tf_op jit(solution)/shard_map/reshape | solution.py:430
  2.7 1.9 %broadcast_select_fusion.live_ref = bf16[384,512]{1,0:T(8,128)(2,1)} fusion(bf16[384,512]{1,0:T(8,128)(2,1)} %param.7, pred[384]{0:T(512)(128)(4,1)S(1)} %broadcast_compare_fusion), kind=kLoop, calls=%fused_computation | loop fusion | flops 196608 | bytes 786816 | tf_op jit(solution)/shard_map/jit(_where)/select_n | solution.py:429
  4.5 77.3 %key_projection_backward.1 = (f32[128,512]{1,0:T(8,128)}, bf16[384,8192]{1,0:T(8,128)(2,1)}) custom-call(bf16[384,8192]{1,0:T(8,128)(2,1)} %x_hbm.1, f32[32,1,256]{2,1,0:T(1,128)} %bitcast.1, bf16[384,512]{1,0:T(8,128)(2,1)} %broadcast_select_fusion.live_ref, bf16[128,512]{1,0:T(8,128)(2,1)} %w_hbm.1), custom_call_target="tpu_custom_call" | custom-call | tf_op jit(solution)/shard_map/key_projection_backward/pallas_call | solution.py:462
  81.8 1.7 %copy.9 = f32[128,512]{1,0:T(8,128)} copy(f32[128,512]{1,0:T(8,128)} %get-tuple-element.4) | data formatting | bytes 524288
  83.4 6.2 %copy.10 = bf16[384,8192]{1,0:T(8,128)(2,1)} copy(bf16[384,8192]{1,0:T(8,128)(2,1)} %get-tuple-element.5) | data formatting | bytes 12582912

commit v2 on v1

v2 whole, which is shorter than its diff:
```python
import jax
import jax.numpy as jnp
from jax import lax
from jax.experimental import pallas as pl
from jax.experimental.pallas import tpu as pltpu
from jax.sharding import PartitionSpec as P

F32 = jnp.float32
BF16 = jnp.bfloat16
NX, NY, NZ = 4, 4, 8
TOK, D, KW, TOKENS = 384, 8192, 512, 98304
CH = 256
NCH = D // CH


def dev(x, y, z, c):
    return {"blk": (y * NZ + z) * 2 + x % 2, "rep": (x // 2) * 2 + c}


class Ring:
    def __init__(self, own, subs, plus, minus, send, recv, ssem, rsem):
        self.own, self.subs, self.to = own, subs, (plus, minus)
        self.send, self.recv, self.ssem, self.rsem = send, recv, ssem, rsem

    def copy(self, i):
        return pltpu.make_async_remote_copy(
            self.send.at[i], self.recv.at[i], self.ssem.at[i], self.rsem.at[i], device_id=self.to[i % 2]
        )

    def put(self, i, rel, h, plus=None):
        for s in range(self.subs):
            v = self.own(rel, h, s)
            if plus is not None:
                v = v + self.recv[plus, s].astype(F32)
            self.send[i, s] = v.astype(self.send.dtype)
        self.copy(i).start()

    def far(self, h):
        self.put(h, 2, h)

    def single(self, d):
        self.put(2 + d, (1, 3)[d], (1, 0)[d])

    def combine(self, d):
        self.copy(d).wait_recv()
        self.put(4 + d, (1, 3)[d], d, plus=d)

    def mine_wait(self, h):
        for i in ((4, 3), (2, 5))[h]:
            self.copy(i).wait_recv()

    def mine(self, h, s):
        a, b = ((4, 3), (2, 5))[h]
        return self.own(0, h, s) + self.recv[a, s].astype(F32) + self.recv[b, s].astype(F32)

    def finish(self):
        for i in range(6):
            self.copy(i).wait_send()


def kernel(
    x_hbm, gain_ref, kc_hbm, seg_ref, w_hbm, wg_ref, X,
    kc_ref, G, live_ref, Wf, Nh, Ns, LT, S, NG, ACC, RB, A2, B2, T, Tb, ZR, O,
    r1x_s, r1x_r, r1y_s, r1y_r, r2y_s, r2y_r, r2x_s, r2x_r,
    xsem, wsem, kcsem, nss, nsr, lts, ltr,
    axs, axr, ays, ayr, zs, zr, shs, shr, sys_, syr,
    q1xs, q1xr, q1ys, q1yr, q2ys, q2yr, q2xs, q2xr,
    zds, zdr, fs, fr,
):
    b, r = lax.axis_index("blk"), lax.axis_index("rep")
    xl, z, y = b % 2, (b // 2) % NZ, b // (2 * NZ)
    xh, c = r // 2, r % 2
    x = 2 * xh + xl
    sib = dev(x, y, z, 1 - c)
    xp, xm = dev((x + 1) % 4, y, z, c), dev((x + 3) % 4, y, z, c)
    yp, ym = dev(x, (y + 1) % 4, z, c), dev(x, (y + 3) % 4, z, c)
    zp, zm = dev(x, y, (z + 1) % 8, c), dev(x, y, (z + 7) % 8, c)
    far_same, far_other = dev((x + 2) % 4, y, z, c), dev((x + 2) % 4, y, z, 1 - c)

    wcp = pltpu.make_async_copy(w_hbm.at[:, pl.ds(pl.multiple_of(256 * c, 256), 256)], Wf.at[c, y, z, xl], wsem)
    wcp.start()
    kcp = pltpu.make_async_copy(kc_hbm, kc_ref, kcsem)
    kcp.start()

    def xcopy(j):
        return pltpu.make_async_copy(x_hbm.at[:, pl.ds(pl.multiple_of(j * CH, CH), CH)], X.at[j], xsem.at[j])

    bar = pltpu.get_barrier_semaphore()
    met = [sib, xp, xm, yp, ym, dev(x, (y + 2) % 4, z, c), far_same, far_other] + [dev(x, y, (z + k) % 8, c) for k in range(1, 8)]
    for d in met:
        pl.semaphore_signal(bar, 1, device_id=d)

    lax.fori_loop(0, NCH, lambda j, u: (xcopy(j).start(), u)[1], 0)
    pl.semaphore_wait(bar, len(met))
    full, h0, h1 = pl.ds(0, 128), pl.ds(0, 64), pl.ds(64, 64)
    cols = ((0, 0), (0, 1), (1, 0), (3, 0), (2, 0), (1, 1), (3, 1), (2, 1))

    def region(col, zz, rows, half=c):
        back, other = cols[col]
        return Wf.at[half, (y + 4 - back) % 4, zz, 1 - xl if other else xl, rows]

    def rcopy(src, dst, ss, rs, to):
        return pltpu.make_async_remote_copy(src, dst, ss, rs, device_id=to)

    def same(ref, ss, rs, to):
        return rcopy(ref, ref, ss, rs, to)

    ax_out = [same(region(0, z, h0), axs.at[0], axr.at[0], xp), same(region(0, z, h1), axs.at[1], axr.at[1], xm)]
    ax_in = [same(region(1, z, h0), axs.at[0], axr.at[0], xp), same(region(1, z, h1), axs.at[1], axr.at[1], xm)]
    def ay(col):
        back, other = cols[col]
        src = region(other, z, full)
        return same(src, ays.at[col - 2], ayr.at[col - 2], dev(x, (y + back) % 4, z, c))

    def ay_in(col):
        return same(region(col, z, full), ays.at[col - 2], ayr.at[col - 2], yp)

    def ay_serve(col):
        ay_in(col).wait_recv()
        z_first(col)
        share_own(col).start()

    def z_at(d, k):
        return (z + 8 - k) % 8 if d == 0 else (z + k) % 8

    def z_out(col, d, k):
        rows = full if k < 4 else (h0, h1)[d]
        return same(region(col, z_at(d, k - 1), rows), zs.at[col, d, k - 1], zr.at[col, d, k - 1], (zp, zm)[d])

    def z_in(col, d, k):
        rows = full if k < 4 else (h0, h1)[d]
        return same(region(col, z_at(d, k), rows), zs.at[col, d, k - 1], zr.at[col, d, k - 1], (zp, zm)[d])

    def share(col, d, k):
        rows = full if k < 4 else (h0, h1)[d]
        return same(region(col, z_at(d, k), rows), shs.at[col, d, k - 1], shr.at[col, d, k - 1], sib)

    def share_in(col, d, k):
        rows = full if k < 4 else (h0, h1)[d]
        return same(region(col, z_at(d, k), rows, 1 - c), shs.at[col, d, k - 1], shr.at[col, d, k - 1], sib)

    def share_own(col):
        return same(region(col, z, full), sys_.at[col], syr.at[col], sib)

    def share_own_in(col):
        return same(region(col, z, full, 1 - c), sys_.at[col], syr.at[col], sib)

    def z_first(col):
        z_out(col, 0, 1).start()
        z_out(col, 1, 1).start()

    def z_serve(k, cols):
        for col in cols:
            for d in range(2):
                z_in(col, d, k).wait_recv()
                if k < 4:
                    z_out(col, d, k + 1).start()
                share(col, d, k).start()

    wcp.wait()
    for cp in ax_out:
        cp.start()
    z_first(0)
    for col in (2, 3, 4):
        ay(col).start()
    share_own(0).start()

    kcp.wait()
    row = jnp.where(seg_ref[...].reshape(1, TOK) != 0, F32(1), F32(0))
    tall = jnp.broadcast_to(row, (128, TOK)).T
    kcv = kc_ref[...].astype(F32)
    live = jnp.where(jnp.concatenate([tall] * 4, axis=1) != 0, kcv, F32(0))
    live_ref[...] = live.astype(BF16)
    LT[:, 0:TOK] = live.T.astype(BF16)
    for j in range(NCH):
        G[j] = gain_ref[CH * j : CH * (j + 1)].astype(F32).reshape(1, CH)
    lt_copy = pltpu.make_async_remote_copy(
        LT.at[:, 0:TOK], LT.at[:, TOK : 2 * TOK], lts, ltr, device_id=sib
    )
    lt_copy.start()

    for cp in ax_in:
        cp.wait_recv()
    z_first(1)
    for col in (5, 6, 7):
        ay(col).start()
    share_own(1).start()

    ACC[...] = jnp.zeros_like(ACC)

    def ssq(g, u):
        tot = jnp.zeros((TOK, 128), F32)
        for i in range(4):
            xcopy(g * 4 + i).wait()
            v = X[g * 4 + i].astype(F32)
            v = v * v
            tot = tot + (v[:, :128] + v[:, 128:])
        ACC[...] += tot
        return u

    lax.fori_loop(0, NCH // 4, ssq, 0)
    mean = jnp.sum(ACC[...], axis=1, keepdims=True) / D
    rstd = lax.rsqrt(mean + 1e-05)
    RB[...] = jnp.broadcast_to(rstd, (TOK, 128))

    for col in (2, 3, 4):
        ay_serve(col)

    def normed(j):
        rb = RB[...]
        v = X[j].astype(F32)
        return (v * jnp.concatenate([rb, rb], axis=1) * G[j]).astype(BF16)

    def n_copy(i):
        return rcopy(Ns.at[i], Nh.at[i, TOK : 2 * TOK], nss.at[i], nsr.at[i], sib)

    def order(i):
        far = i < 2
        mid = i < 10
        yy = jnp.where(far, (y + 2) % 4, jnp.where(mid, (i - 2) % 4, (y + jnp.where(i < 12, 1, jnp.where(i < 14, 3, 0))) % 4))
        zz = jnp.where(far, 2 + i, jnp.where(mid, (i - 2) // 4, 2 + i % 2))
        return yy, zz

    def norm_sib(i, u):
        yy, zz = order(i)
        Ns[yy * 4 + zz] = normed(yy * 8 + 4 * (1 - c) + zz)
        n_copy(yy * 4 + zz).start()
        return u

    def norm_own(i, u):
        yy, zz = order(i)
        Nh[yy * 4 + zz, 0:TOK] = normed(yy * 8 + 4 * c + zz)
        return u

    lax.fori_loop(0, 16, norm_sib, 0)
    for col in (5, 6, 7):
        ay_serve(col)
    lax.fori_loop(0, 16, norm_own, 0)
    lt_copy.wait_recv()

    def product(i, u):
        yy, zz = order(i)
        at = yy * 4 + zz
        n_copy(at).wait_recv()
        st = jnp.dot(LT[...], Nh[at], preferred_element_type=F32)
        S[at, 0] = st[:, :128]
        S[at, 1] = st[:, 128:]
        return u

    def x_of(rel):
        xx = (x + rel) % 4
        return xx % 2, xx // 2

    def part(first, b):
        return pl.ds(pl.multiple_of(first + 128 * b, 128), 128)

    def rings(b):
        def own_1x(rel, h, s):
            l, hi = x_of(rel)
            return S[s * 4 + h, l, part(256 * hi, b)]

        def own_1y(rel, h, s):
            return S[((y + rel) % 4) * 4 + 2 + h, s // 2, part(256 * (s % 2), b)]

        def own_2y(rel, h, s):
            return A2[h, (y + rel) % 4, part(0, b)]

        def own_2x(rel, h, s):
            l, hi = x_of(rel)
            return B2[h, l * 2 + hi, part(0, b)]

        return (
            Ring(own_1x, 4, xp, xm, r1x_s.at[b], r1x_r.at[b], q1xs.at[b], q1xr.at[b]),
            Ring(own_1y, 4, yp, ym, r1y_s.at[b], r1y_r.at[b], q1ys.at[b], q1yr.at[b]),
            Ring(own_2x, 1, xp, xm, r2x_s.at[b], r2x_r.at[b], q2xs.at[b], q2xr.at[b]),
            Ring(own_2y, 1, yp, ym, r2y_s.at[b], r2y_r.at[b], q2ys.at[b], q2yr.at[b]),
        )

    every = [rings(0), rings(1)]

    def far(ring):
        ring.far(0)
        ring.far(1)

    def single(ring):
        ring.single(0)
        ring.single(1)

    def combine(ring):
        ring.combine(0)
        ring.combine(1)

    def zd_copy(k, b):
        return rcopy(Tb.at[k, part(0, b)], ZR.at[z, part(0, b)], zds.at[b, k], zdr.at[b, z], dev(x, y, 4 * c + k, c))

    def third(b):
        _, _, r2x, r2y = every[b]
        for h in range(2):
            r2y.mine_wait(h)
            T[h, part(0, b)] = r2y.mine(h, 0)
            r2x.mine_wait(h)
            T[2 + h, part(0, b)] = r2x.mine(h, 0)
        for k in range(4):
            @pl.when(4 * c + k != z)
            def _(k=k):
                Tb[k, part(0, b)] = T[k, part(0, b)].astype(BF16)
                zd_copy(k, b).start()

    owner = z // 4 == c

    def out_copy(i, b):
        to = (sib, far_same, far_other)[i]
        return rcopy(O.at[xh, b], O.at[xh, b], fs.at[b, i], fr.at[b, jnp.where(i == 0, 0, 1)], to)

    def fourth(b):
        @pl.when(owner)
        def _():
            for s in range(8):
                @pl.when(s != z)
                def _(s=s):
                    rcopy(Tb.at[0, part(0, b)], ZR.at[s, part(0, b)], zds.at[b, 0], zdr.at[b, s], sib).wait_recv()
            ZR[z, part(0, b)] = jnp.zeros((128, 128), BF16)
            tot = T[z % 4, part(0, b)]
            for s in range(8):
                tot = tot + ZR[s, part(0, b)].astype(F32)
            O[xh, b] = (tot / jnp.sqrt(F32(TOKENS))).T
            for i in range(3):
                out_copy(i, b).start()

    r1x, r1y, r2x, r2y = every[0]
    q1x, q1y, q2x, q2y = every[1]
    lax.fori_loop(0, 2, product, 0)
    far(r1y)
    lax.fori_loop(2, 6, product, 0, unroll=2)
    r1x.far(0)
    z_serve(1, (0, 1, 2))
    lax.fori_loop(6, 10, product, 0, unroll=2)
    r1x.far(1)
    single(r1x)
    lax.fori_loop(10, 16, product, 0, unroll=2)
    single(r1y)
    z_serve(1, (3, 4, 5))
    combine(r1y)
    far(q1y)
    single(q1y)
    combine(r1x)
    far(q1x)
    single(q1x)
    z_serve(1, (6, 7))

    ACC[...] = jnp.zeros_like(ACC)

    def ng_chunk(yy, zz):
        j = yy * 8 + zz
        nt = (((1,), (1,)), ((), ()))
        ng = lax.dot_general(live_ref[:, 0:256], Wf[0, yy, zz].reshape(CH, 256), nt, preferred_element_type=F32)
        ng += lax.dot_general(live_ref[:, 256:512], Wf[1, yy, zz].reshape(CH, 256), nt, preferred_element_type=F32)
        NG[j] = ng
        v = X[j].astype(F32) * G[j] * ng
        ACC[...] += v[:, :128] + v[:, 128:]

    def ng_chunks(zz):
        lax.fori_loop(0, 4, lambda yy, u: (ng_chunk(yy, zz), u)[1], 0, unroll=True)

    def ng_step(k):
        for col in range(8):
            for d in range(2):
                share_in(col, d, k).wait_recv()
        for d in range(2 if k < 4 else 1):
            ng_chunks(z_at(d, k))

    def second(rings_b, b, along_y):
        r1x, r1y, r2x, r2y = rings_b
        one, two, to = (r1y, r2x, B2) if along_y else (r1x, r2y, A2)
        for h in range(2):
            one.mine_wait(h)
            for s in range(4):
                to[h, s, part(0, b)] = one.mine(h, s)
        far(two)
        single(two)

    combine(q1y)
    second(every[0], 0, True)
    z_serve(2, (0, 1, 2))
    combine(q1x)
    second(every[0], 0, False)
    z_serve(2, (3, 4, 5))
    for col in range(8):
        share_own_in(col).wait_recv()
    ng_chunks(z)
    combine(r2x)
    combine(r2y)
    z_serve(2, (6, 7))
    ng_step(1)
    second(every[1], 1, True)
    second(every[1], 1, False)
    z_serve(3, (0, 1, 2))
    ng_step(2)
    third(0)
    z_serve(3, (3, 4, 5))
    combine(q2x)
    combine(q2y)
    z_serve(3, (6, 7))
    ng_step(3)
    third(1)
    fourth(0)
    z_serve(4, range(8))
    ng_step(4)
    fourth(1)

    inner = jnp.sum(ACC[...], axis=1, keepdims=True)
    rb = RB[...]
    ACC[...] = rb * rb * rb * jnp.broadcast_to(inner, (TOK, 128)) / D

    def last(j, u):
        rb, co = RB[...], ACC[...]
        v = X[j].astype(F32)
        g = G[j]
        out = jnp.concatenate([rb, rb], axis=1) * g * NG[j] - v * jnp.concatenate([co, co], axis=1)
        X[j] = out.astype(BF16)
        return u

    lax.fori_loop(0, NCH, last, 0)

    for b in range(2):
        @pl.when(jnp.logical_not(owner))
        def _(b=b):
            rcopy(O.at[xh, b], O.at[xh, b], fs.at[b, 0], fr.at[b, 0], sib).wait_recv()

        rcopy(O.at[1 - xh, b], O.at[1 - xh, b], fs.at[b, 1], fr.at[b, 1], far_same).wait_recv()
        wg_ref[:, 128 * b : 128 * b + 128] = O[0, b]
        wg_ref[:, 256 + 128 * b : 384 + 128 * b] = O[1, b]

        @pl.when(owner)
        def _(b=b):
            for i in range(3):
                out_copy(i, b).wait_send()

        for k in range(4):
            @pl.when(4 * c + k != z)
            def _(k=k, b=b):
                zd_copy(k, b).wait_send()
        for ring in every[b]:
            ring.finish()
    for cp in ax_out:
        cp.wait_send()
    for col in range(2, 8):
        ay(col).wait_send()
    for col in range(8):
        for d in range(2):
            for k in range(1, 5):
                z_out(col, d, k).wait_send()
                share(col, d, k).wait_send()
    for col in range(8):
        share_own(col).wait_send()
    lt_copy.wait_send()
    lax.fori_loop(0, 16, lambda i, u: (n_copy(i).wait_send(), u)[1], 0)


def copy_out(ig, wg, ig_out, wg_out, sem):
    cps = [pltpu.make_async_copy(ig.at[j], ig_out.at[:, pl.ds(j * CH, CH)], sem.at[j]) for j in range(NCH)]
    cps.append(pltpu.make_async_copy(wg, wg_out, sem.at[NCH]))
    for cp in cps:
        cp.start()
    for cp in cps:
        cp.wait()


def on_device(layer_input, norm_gain, key_cotangent, segment_ids, key_weight):
    dma = pltpu.SemaphoreType.DMA
    vm = pltpu.VMEM

    def ring(subs, dtype):
        return [vm((2, 6, subs, 128, 128), dtype)] * 2

    scratch = [
        vm((TOK, KW), BF16),
        vm((NCH, 1, CH), F32),
        vm((TOK, KW), BF16),
        vm((2, NY, NZ, 2, 128, 256), BF16),
        vm((16, 2 * TOK, CH), BF16),
        vm((16, TOK, CH), BF16),
        vm((KW, 2 * TOK), BF16),
        vm((16, 2, KW, 128), F32),
        vm((NCH, TOK, CH), F32),
        vm((TOK, 128), F32),
        vm((TOK, 128), F32),
        vm((2, 4, 256, 128), F32),
        vm((2, 4, 256, 128), F32),
        vm((4, 256, 128), F32),
        vm((4, 256, 128), BF16),
        vm((8, 256, 128), BF16),
        vm((2, 2, 128, 128), F32),
        *ring(4, BF16), *ring(4, BF16), *ring(1, F32), *ring(1, F32),
        dma((NCH,)), dma, dma, dma((16,)), dma((16,)), dma, dma,
        dma((2,)), dma((2,)), dma((6,)), dma((6,)),
        dma((8, 2, 4)), dma((8, 2, 4)), dma((8, 2, 4)), dma((8, 2, 4)), dma((8,)), dma((8,)),
        *[dma((2, 6))] * 8,
        dma((2, 4)), dma((2, 8)), dma((2, 3)), dma((2, 2)),
    ]
    anyspace = pl.BlockSpec(memory_space=pl.ANY)
    vspace = pl.BlockSpec(memory_space=pltpu.VMEM)
    wg, ig = pl.pallas_call(
        kernel,
        name="key_projection_backward",
        out_shape=(pltpu.VMEM((128, KW), F32), pltpu.VMEM((NCH, TOK, CH), BF16)),
        in_specs=[anyspace, vspace, anyspace, vspace, anyspace],
        out_specs=(vspace, vspace),
        scratch_shapes=scratch,
        compiler_params=pltpu.CompilerParams(
            collective_id=0, has_side_effects=True, vmem_limit_bytes=53 * 2**20
        ),
    )(layer_input, norm_gain, key_cotangent, segment_ids, key_weight)
    ig, wg = pl.pallas_call(
        copy_out,
        name="copy_out",
        out_shape=(jax.ShapeDtypeStruct((TOK, D), BF16), jax.ShapeDtypeStruct((128, KW), F32)),
        in_specs=[vspace] * 2,
        out_specs=(anyspace,) * 2,
        scratch_shapes=[dma((NCH + 1,))],
        compiler_params=pltpu.CompilerParams(vmem_limit_bytes=2**20),
    )(pltpu.with_memory_space_constraint(ig, pltpu.VMEM), pltpu.with_memory_space_constraint(wg, pltpu.VMEM))
    return wg, ig


def solution(mesh):
    placed = (
        P(("blk", "rep"), None),
        P(),
        P(("blk", "rep"), None),
        P(("blk", "rep")),
        P("blk", None),
    )
    return jax.shard_map(
        on_device,
        mesh=mesh,
        in_specs=placed,
        out_specs=(P("blk", None), P(("blk", "rep"), None)),
        check_vma=False,
    )
```

time: 89.9 us -> 74.8 us (0.83)
  local copies, waits for them, and re-layouts: 7.87 us -> 0 us
  other arithmetic: 3.88 us -> 0 us
  Pallas kernels: 77.3 us -> 74 us
    unnamed x2 -> x0, local copies, waits for them, and re-layouts: 7.87 us -> none
    pallas_call x1 -> x2, Pallas kernels: 77.3 us -> 74 us  [the longest x1 71 us: on_device(): pl.pallas_call(kernel, name='key_projection_backward', out_shape=(pltpu.V...]
    select_n x1 -> x0, other arithmetic: 1.86 us -> none  [on_device(): jnp.where((segment_ids != 0)[:, None], key_cotangent, jnp.zeros_like(key_...]
    reshape x1 -> x0, other arithmetic: 1.33 us -> none  [on_device(): gain = norm_gain.astype(F32).reshape(NCH, 1, CH)]
where the time goes in v2:
time: 74.8 us; the launch traced here: 74.6 us
  Pallas kernels  74 us (99%)
    pallas_call x1, Pallas kernels, on_device(): pl.pallas_call(kernel, name='key_projection_backward', out_shape=(pltpu.V...  71 us
    pallas_call x1, Pallas kernels, on_device(): pl.pallas_call(copy_out, name='copy_out', out_shape=(jax.ShapeDtypeStruct...  3 us

profile of v2, /device:TPU:1, one launch (start us, length us, event | category | flops | bytes accessed | tf_op | source)
XLA Modules:
  0.0 74.6 jit_solution(388784288838867192)
XLA Ops:
  0.6 71.0 %key_projection_backward.1 = (f32[128,512]{1,0:T(8,128)S(1)}, bf16[32,384,256]{2,1,0:T(8,128)(2,1)S(1)}) custom-call(bf16[384,8192]{1,0:T(8,128)(2,1)} %x_hbm.1, bf16[8192]{0:T(1024)(128)(2,1)} %gain_ref.1, bf16[384,512]{1,0:T(8,128)(2,1)} %kc_hbm.1, s32[384]{0:T(512)} %seg_ref.1, bf16[128,512]{1,0:T(8,128)(2,1)} %w_hbm.1), custom_call_target="tpu_custom_call" | custom-call | tf_op jit(solution)/shard_map/key_projection_backward/pallas_call | solution.py:503
  71.6 3.0 %copy_out.1 = (bf16[384,8192]{1,0:T(8,128)(2,1)}, f32[128,512]{1,0:T(8,128)}) custom-call(bf16[32,384,256]{2,1,0:T(8,128)(2,1)S(1)} %get-tuple-element.6.ig, f32[128,512]{1,0:T(8,128)S(1)} %get-tuple-element.7.wg), custom_call_target="tpu_custom_call" | custom-call | tf_op jit(solution)/shard_map/copy_out/pallas_call | solution.py:514

commit v3 on v2

--- a/solution.py
+++ b/solution.py
@@ -11,6 +11,7 @@
 TOK, D, KW, TOKENS = 384, 8192, 512, 98304
 CH = 256
 NCH = D // CH
+AHEAD = 6
 
 
 def dev(x, y, z, c):
@@ -23,16 +24,19 @@
         self.send, self.recv, self.ssem, self.rsem = send, recv, ssem, rsem
 
     def copy(self, i):
-        return pltpu.make_async_remote_copy(
-            self.send.at[i], self.recv.at[i], self.ssem.at[i], self.rsem.at[i], device_id=self.to[i % 2]
-        )
+        src, dst = (bufs[i // 4].at[i % 4] for bufs in (self.send, self.recv))
+        return pltpu.make_async_remote_copy(src, dst, self.ssem.at[i], self.rsem.at[i], device_id=self.to[i % 2])
+
+    def got(self, i, s):
+        return self.recv[i // 4][i % 4, s].astype(F32)
 
     def put(self, i, rel, h, plus=None):
         for s in range(self.subs):
             v = self.own(rel, h, s)
             if plus is not None:
-                v = v + self.recv[plus, s].astype(F32)
-            self.send[i, s] = v.astype(self.send.dtype)
+                v = v + self.got(plus, s)
+            ref = self.send[i // 4]
+            ref[i % 4, s] = v.astype(ref.dtype)
         self.copy(i).start()
 
     def far(self, h):
@@ -51,7 +55,7 @@
 
     def mine(self, h, s):
         a, b = ((4, 3), (2, 5))[h]
-        return self.own(0, h, s) + self.recv[a, s].astype(F32) + self.recv[b, s].astype(F32)
+        return self.own(0, h, s) + self.got(a, s) + self.got(b, s)
 
     def finish(self):
         for i in range(6):
@@ -62,6 +66,7 @@
     x_hbm, gain_ref, kc_hbm, seg_ref, w_hbm, wg_ref, X,
     kc_ref, G, live_ref, Wf, Nh, Ns, LT, S, NG, ACC, RB, A2, B2, T, Tb, ZR, O,
     r1x_s, r1x_r, r1y_s, r1y_r, r2y_s, r2y_r, r2x_s, r2x_r,
+    c1x_s, c1x_r, c1y_s, c1y_r, c2y_s, c2y_r, c2x_s, c2x_r,
     xsem, wsem, kcsem, nss, nsr, lts, ltr,
     axs, axr, ays, ayr, zs, zr, shs, shr, sys_, syr,
     q1xs, q1xr, q1ys, q1yr, q2ys, q2yr, q2xs, q2xr,
@@ -232,10 +237,13 @@
         Nh[yy * 4 + zz, 0:TOK] = normed(yy * 8 + 4 * c + zz)
         return u
 
-    lax.fori_loop(0, 16, norm_sib, 0)
+    def norm_both(i, u):
+        norm_sib(i, u)
+        return norm_own(i, u)
+
+    lax.fori_loop(0, AHEAD, norm_both, 0)
     for col in (5, 6, 7):
         ay_serve(col)
-    lax.fori_loop(0, 16, norm_own, 0)
     lt_copy.wait_recv()
 
     def product(i, u):
@@ -270,10 +278,10 @@
             return B2[h, l * 2 + hi, part(0, b)]
 
         return (
-            Ring(own_1x, 4, xp, xm, r1x_s.at[b], r1x_r.at[b], q1xs.at[b], q1xr.at[b]),
-            Ring(own_1y, 4, yp, ym, r1y_s.at[b], r1y_r.at[b], q1ys.at[b], q1yr.at[b]),
-            Ring(own_2x, 1, xp, xm, r2x_s.at[b], r2x_r.at[b], q2xs.at[b], q2xr.at[b]),
-            Ring(own_2y, 1, yp, ym, r2y_s.at[b], r2y_r.at[b], q2ys.at[b], q2yr.at[b]),
+            Ring(own_1x, 4, xp, xm, (r1x_s.at[b], c1x_s.at[b]), (r1x_r.at[b], c1x_r.at[b]), q1xs.at[b], q1xr.at[b]),
+            Ring(own_1y, 4, yp, ym, (r1y_s.at[b], c1y_s.at[b]), (r1y_r.at[b], c1y_r.at[b]), q1ys.at[b], q1yr.at[b]),
+            Ring(own_2x, 1, xp, xm, (r2x_s.at[b], c2x_s.at[b]), (r2x_r.at[b], c2x_r.at[b]), q2xs.at[b], q2xr.at[b]),
+            Ring(own_2y, 1, yp, ym, (r2y_s.at[b], c2y_s.at[b]), (r2y_r.at[b], c2y_r.at[b]), q2ys.at[b], q2yr.at[b]),
         )
 
     every = [rings(0), rings(1)]
@@ -329,12 +337,17 @@
 
     r1x, r1y, r2x, r2y = every[0]
     q1x, q1y, q2x, q2y = every[1]
-    lax.fori_loop(0, 2, product, 0)
+
+    def step(i, u):
+        product(i, u)
+        return norm_both(i + AHEAD, u)
+
+    lax.fori_loop(0, 2, step, 0)
     far(r1y)
-    lax.fori_loop(2, 6, product, 0, unroll=2)
+    lax.fori_loop(2, 6, step, 0)
     r1x.far(0)
     z_serve(1, (0, 1, 2))
-    lax.fori_loop(6, 10, product, 0, unroll=2)
+    lax.fori_loop(6, 10, step, 0)
     r1x.far(1)
     single(r1x)
     lax.fori_loop(10, 16, product, 0, unroll=2)
@@ -343,10 +356,10 @@
     combine(r1y)
     far(q1y)
     single(q1y)
+    z_serve(1, (6, 7))
     combine(r1x)
     far(q1x)
     single(q1x)
-    z_serve(1, (6, 7))
 
     ACC[...] = jnp.zeros_like(ACC)
 
@@ -380,33 +393,33 @@
         single(two)
 
     combine(q1y)
+    z_serve(2, (0, 1, 2))
     second(every[0], 0, True)
-    z_serve(2, (0, 1, 2))
     combine(q1x)
+    z_serve(2, (3, 4, 5))
     second(every[0], 0, False)
-    z_serve(2, (3, 4, 5))
+    combine(r2x)
+    z_serve(2, (6, 7))
+    combine(r2y)
     for col in range(8):
         share_own_in(col).wait_recv()
     ng_chunks(z)
-    combine(r2x)
-    combine(r2y)
-    z_serve(2, (6, 7))
-    ng_step(1)
     second(every[1], 1, True)
     second(every[1], 1, False)
+    ng_step(1)
+    third(0)
     z_serve(3, (0, 1, 2))
-    ng_step(2)
-    third(0)
-    z_serve(3, (3, 4, 5))
     combine(q2x)
     combine(q2y)
+    ng_step(2)
+    third(1)
+    z_serve(3, (3, 4, 5))
     z_serve(3, (6, 7))
+    fourth(0)
     ng_step(3)
-    third(1)
-    fourth(0)
+    fourth(1)
     z_serve(4, range(8))
     ng_step(4)
-    fourth(1)
 
     inner = jnp.sum(ACC[...], axis=1, keepdims=True)
     rb = RB[...]
@@ -470,8 +483,11 @@
     dma = pltpu.SemaphoreType.DMA
     vm = pltpu.VMEM
 
-    def ring(subs, dtype):
-        return [vm((2, 6, subs, 128, 128), dtype)] * 2
+    def ring(subs, dtype=BF16):
+        return [vm((2, 4, subs, 128, 128), dtype)] * 2
+
+    def last(subs, dtype):
+        return [vm((2, 2, subs, 128, 128), dtype)] * 2
 
     scratch = [
         vm((TOK, KW), BF16),
@@ -491,7 +507,8 @@
         vm((4, 256, 128), BF16),
         vm((8, 256, 128), BF16),
         vm((2, 2, 128, 128), F32),
-        *ring(4, BF16), *ring(4, BF16), *ring(1, F32), *ring(1, F32),
+        *ring(4), *ring(4), *ring(1, F32), *ring(1, F32),
+        *last(4, BF16), *last(4, BF16), *last(1, F32), *last(1, F32),
         dma((NCH,)), dma, dma, dma((16,)), dma((16,)), dma, dma,
         dma((2,)), dma((2,)), dma((6,)), dma((6,)),
         dma((8, 2, 4)), dma((8, 2, 4)), dma((8, 2, 4)), dma((8, 2, 4)), dma((8,)), dma((8,)),

time: 74.8 us -> 74.7 us (level)
  no operation moved by 1% of the time
where the time goes in v3:
time: 74.7 us; the launch traced here: 74.6 us
  Pallas kernels  73.9 us (99%)
    pallas_call x1, Pallas kernels, on_device(): pl.pallas_call(kernel, name='key_projection_backward', out_shape=(pltpu.V...  70.9 us
    pallas_call x1, Pallas kernels, on_device(): pl.pallas_call(copy_out, name='copy_out', out_shape=(jax.ShapeDtypeStruct...  3 us

profile of v3, /device:TPU:1, one launch (start us, length us, event | category | flops | bytes accessed | tf_op | source)
XLA Modules:
  0.0 74.6 jit_solution(8617456716686455106)
XLA Ops:
  0.6 70.9 %key_projection_backward.1 = (f32[128,512]{1,0:T(8,128)S(1)}, bf16[32,384,256]{2,1,0:T(8,128)(2,1)S(1)}) custom-call(bf16[384,8192]{1,0:T(8,128)(2,1)} %x_hbm.1, bf16[8192]{0:T(1024)(128)(2,1)} %gain_ref.1, bf16[384,512]{1,0:T(8,128)(2,1)} %kc_hbm.1, s32[384]{0:T(512)} %seg_ref.1, bf16[128,512]{1,0:T(8,128)(2,1)} %w_hbm.1), custom_call_target="tpu_custom_call" | custom-call | tf_op jit(solution)/shard_map/key_projection_backward/pallas_call | solution.py:520
  71.6 3.0 %copy_out.1 = (bf16[384,8192]{1,0:T(8,128)(2,1)}, f32[128,512]{1,0:T(8,128)}) custom-call(bf16[32,384,256]{2,1,0:T(8,128)(2,1)S(1)} %get-tuple-element.6.ig, f32[128,512]{1,0:T(8,128)S(1)} %get-tuple-element.7.wg), custom_call_target="tpu_custom_call" | custom-call | tf_op jit(solution)/shard_map/copy_out/pallas_call | solution.py:531
